TPU v7x, 32 devices: a whole 2x2x4 slice. The times are simulated.
32 devices in a mesh: batch: 2 (over y), expert: 16 (over z, x, core).
Axes of the slice: x: 2, y: 2, z: 4, core: 2. Of those that a mesh axis runs over, the one named last changes fastest.
Arguments:
- resid: bfloat16 [1024, 2048], P(('batch', 'expert')), may hold values from -6 to 6
- queries: bfloat16 [1024, 2048], P(('batch', 'expert')), may hold values from -6 to 6
- enc_keys: bfloat16 [32, 32, 2048], P(('batch', 'expert')), may hold values from -6 to 6
- enc_values: bfloat16 [32, 32, 2048], P(('batch', 'expert')), may hold values from -6 to 6
- src_lengths: int32 [32], P(('batch', 'expert')), may hold values from 2 to 32, as said below
- ln_gain: float32 [2048], replicated, may hold values from 0.5 to 1.5
- router: bfloat16 [2048, 16], replicated, may hold values from -0.125 to 0.125
- w_in: bfloat16 [16, 2048, 4096], P('expert', None, 'batch'), may hold values from -0.125 to 0.125
- w_out: bfloat16 [16, 4096, 2048], P('expert', 'batch'), may hold values from -0.09375 to 0.09375
- expert_ids: int32 [1024, 2], P(('batch', 'expert')), may hold values from 0 to 15, all different within a row; in each aligned block of 32 rows (0 to 31, 32 to 63, ...) at most 8 rows name the same one
Outputs:
- mixed: bfloat16 [1024, 2048], P(('batch', 'expert'))
Inputs may be any that keep to these rules, and one draw needn't show every extreme that they name: `expert_ids`: each row names two different experts. In each aligned block of 32 rows (the rows of one device) no expert is named more than 8 times, a bound that some block reaches. `src_lengths`: some source sentence has all 32 positions valid.
All inputs are finite; a program needn't handle non-finite values.
Results may differ from a plain program's by a relative error of at most 0.005.
Values may be sent and summed in bfloat16 or wider, within the bound.
A program may use at most 64 MiB of HBM per device.

v0:
```python
import math

import jax
import jax.numpy as jnp
from jax import lax
from jax.sharding import PartitionSpec as P

D = 2048
HEADS = 16
HEAD_DIM = 128


def expert_term(inputs, first_weight, second_weight):
    hidden = jnp.maximum(
        jnp.dot(inputs, first_weight, preferred_element_type=jnp.float32), 0.0
    ).astype(jnp.bfloat16)
    return jnp.dot(hidden, second_weight, preferred_element_type=jnp.float32)


def on_device(
    resid, queries, enc_keys, enc_values, src_lengths, ln_gain, router, w_in, w_out, expert_ids
):
    row_count = resid.shape[0]
    key_count = enc_keys.shape[1]
    query_heads = queries.reshape(row_count, HEADS, HEAD_DIM)
    key_heads = enc_keys.reshape(key_count, HEADS, HEAD_DIM)
    value_heads = enc_values.reshape(key_count, HEADS, HEAD_DIM)
    scores = jnp.einsum(
        "rhd,thd->hrt", query_heads, key_heads, preferred_element_type=jnp.float32
    ) / math.sqrt(HEAD_DIM)
    visible = jnp.arange(key_count, dtype=jnp.int32) < src_lengths[0]
    scores = jnp.where(visible[None, None, :], scores, -1e30)
    top_score = jnp.max(scores, axis=-1, keepdims=True)
    powers = jnp.exp(scores - top_score)
    weights = (powers / jnp.sum(powers, axis=-1, keepdims=True)).astype(jnp.bfloat16)
    context = jnp.einsum(
        "hrt,thd->rhd", weights, value_heads, preferred_element_type=jnp.float32
    ).reshape(row_count, D)
    summed = resid.astype(jnp.float32) + context
    center = jnp.mean(summed, axis=-1, keepdims=True)
    spread = jnp.mean((summed - center) ** 2, axis=-1, keepdims=True)
    normed = ((summed - center) * lax.rsqrt(spread + 1e-05) * ln_gain).astype(jnp.bfloat16)
    experts_all = router.shape[1]
    capacity = max(2, 4 * row_count // experts_all)
    logits = jnp.dot(normed, router, preferred_element_type=jnp.float32)
    flat_expert = expert_ids.reshape(-1)
    onehot = (flat_expert[:, None] == jnp.arange(experts_all, dtype=jnp.int32)[None, :]).astype(
        jnp.int32
    )
    before = jnp.cumsum(onehot, axis=0) - onehot
    slots = jnp.sum(before * onehot, axis=1)
    flat_owner = flat_expert * capacity + slots
    chosen = jnp.sum(
        onehot.reshape(row_count, 2, experts_all).astype(jnp.float32) * logits[:, None, :], axis=-1
    )
    gates = jax.nn.sigmoid(chosen)
    assigned = jnp.repeat(normed, 2, axis=0)
    outgoing = jnp.zeros((experts_all * capacity, D), jnp.bfloat16).at[flat_owner].set(assigned)
    outgoing = outgoing.reshape(experts_all, capacity, D)
    first_weight = w_in[0]
    second_weight = w_out[0]
    stacked = lax.all_gather(outgoing[:, None], "batch", axis=1, tiled=True)
    arrived = lax.all_to_all(stacked, "expert", split_axis=0, concat_axis=0, tiled=True)
    sources = arrived.shape[0]
    item_count = arrived.shape[1]
    partial_value = expert_term(arrived.reshape(-1, D), first_weight, second_weight)
    outbound = partial_value.astype(jnp.bfloat16).reshape(sources, item_count, capacity, D)
    returned_parts = lax.all_to_all(outbound, "expert", split_axis=0, concat_axis=0, tiled=True)
    totals = lax.psum_scatter(
        returned_parts.astype(jnp.float32).astype(jnp.bfloat16),
        "batch",
        scatter_dimension=1,
        tiled=True,
    )
    expert_out = totals.reshape(experts_all * capacity, D)
    returned = jnp.take(expert_out, flat_owner, axis=0).astype(jnp.float32).reshape(row_count, 2, D)
    mixed = summed + jnp.sum(gates[:, :, None] * returned, axis=1)
    return mixed.astype(jnp.bfloat16)


def solution(mesh):
    return jax.shard_map(
        on_device,
        mesh=mesh,
        in_specs=(
            P(("batch", "expert"), None),
            P(("batch", "expert"), None),
            P(("batch", "expert"), None, None),
            P(("batch", "expert"), None, None),
            P(("batch", "expert")),
            P(),
            P(),
            P("expert", None, "batch"),
            P("expert", "batch", None),
            P(("batch", "expert"), None),
        ),
        out_specs=P(("batch", "expert"), None),
        check_vma=False,
    )
```

profile of v0, /device:TPU:0, one launch (start us, length us, event | category | flops | bytes accessed | tf_op | source)
XLA Modules:
  0.0 163.4 jit_solution(10269189838275672676)
XLA Ops:
  6.5 0.0 copy-start
  6.5 0.0 all-gather.2.cloned.1.call-start
  6.5 0.7 broadcast_multiply_fusion
  7.3 0.8 copy.51
  8.7 0.1 copy.54
  8.8 0.1 mul.64
  8.9 0.1 reshape.109
  9.0 0.1 fusion.26
  9.1 0.1 reduce_window_sum.11
  9.2 0.2 select_reduce_fusion
  9.3 0.9 copy.60
  10.3 0.9 copy.61
  11.2 0.0 copy-done
  11.2 0.2 fusion.34
  11.5 0.2 convolution_bitcast_fusion
  11.7 1.0 fusion.33
  12.8 1.1 multiply_reduce_fusion.1
  13.9 1.0 multiply_convert_fusion
  14.9 0.1 broadcast_in_dim.42
  15.1 0.1 reshape.126
  15.2 1.8 %scatter_custom_fusion = bf16[128,2048]{1,0:T(8,128)(2,1)} fusion(s32[64]{0:T(128)S(1)} %fusion.27, bf16[64,2048]{1,0:T(8,128)(2,1)S(1)} %reshape.126, bf16[]{:T(256)} %constant.43.clone.1), kind=kCustom, calls=%fused_computation.20 | custom fusion | bytes 524290 | tf_op jit(solution)/shard_map/scatter | solution.py:58
  17.0 0.0 all-gather.2.cloned.1.call-update
  17.0 0.0 all-reduce.3.cloned.1.call-start
  17.1 24.1 %all-gather.2.cloned.1.call-done = bf16[16,2,8,2048]{3,2,1,0:T(8,128)(2,1)} async-done(((bf16[16,1,8,2048]{3,2,1,0:T(8,128)(2,1)}), bf16[16,2,8,2048]{3,2,1,0:T(8,128)(2,1)}) %all-gather.2.cloned.1.call-update) | async-done | bytes 1048592 | tf_op jit(solution)/shard_map/all_gather | solution.py:62
  41.2 30.5 %all_to_all.10 = bf16[16,2,8,2048]{3,2,1,0:T(8,128)(2,1)S(1)} all-to-all(bf16[16,2,8,2048]{3,2,1,0:T(8,128)(2,1)} %all-gather.2.cloned.1.call-done), channel_id=1, replica_groups=mesh['batch'=2,'expert'=16] {'expert'}, dimensions={0} | all-to-all | bytes 2097152 | tf_op jit(solution)/shard_map/all_to_all | solution.py:63
  71.7 0.0 copy-start.3
  71.7 0.0 copy-start.2
  71.7 0.0 copy-start.4
  71.7 0.0 copy-start.1
  71.7 10.3 %fusion.11 = bf16[256,2048]{1,0:T(8,128)(2,1)S(1)} fusion(bf16[1,2048,2048]{2,1,0:T(8,128)(2,1)} %param.18, bf16[256,2048]{1,0:T(8,128)(2,1)S(1)} %bitcast.66, bf16[1,2048,2048]{2,1,0:T(8,128)(2,1)} %param.17), kind=kOutput, calls=%fused_computation.9 | convolution fusion | flops 4296540160 | bytes 18874368 | tf_op jit(solution)/shard_map/dot_general | solution.py:17
  82.0 29.7 %all_to_all.11 = bf16[16,2,8,2048]{3,2,1,0:T(8,128)(2,1)} all-to-all(bf16[16,2,8,2048]{3,2,1,0:T(8,128)(2,1)S(1)} %bitcast.67), channel_id=1, replica_groups=mesh['batch'=2,'expert'=16] {'expert'}, dimensions={0} | all-to-all | bytes 2097152 | tf_op jit(solution)/shard_map/all_to_all | solution.py:68
  111.8 0.0 all-reduce.3.cloned.1.call-update
  111.8 0.1 reduce_sum.63
  111.9 0.1 copy.52
  112.0 0.0 copy-done.3
  112.0 0.1 copy.53
  112.1 0.0 copy-done.2
  112.1 0.2 fusion.39
  112.3 0.1 copy.50
  112.4 0.0 copy-done.4
  112.4 0.6 dynamic-slice
  113.0 38.4 %all-reduce.3.cloned.1.call-done = bf16[16,2,8,2048]{3,2,1,0:T(8,128)(2,1)} async-done(((bf16[16,2,8,2048]{3,2,1,0:T(8,128)(2,1)}), bf16[16,2,8,2048]{3,2,1,0:T(8,128)(2,1)}) %all-reduce.3.cloned.1.call-update) | async-done | bytes 1048592
  151.4 1.7 %dynamic-slice_bitcast_fusion = bf16[128,2048]{1,0:T(8,128)(2,1)S(1)} fusion(bf16[16,2,8,2048]{3,2,1,0:T(8,128)(2,1)} %all-reduce.3.cloned.1.call-done, u32[]{:T(128)} %bitcast.12), kind=kLoop, calls=%fused_computation.15 | loop fusion | bytes 1048580 | tf_op jit(solution)/shard_map/reshape | solution.py:75
  153.1 0.7 gather_fusion
  153.9 0.2 gather.7
  154.1 1.7 %multiply_reduce_fusion = f32[32,2048]{1,0:T(8,128)S(1)} fusion(bf16[32,2,2048]{2,1,0:T(2,128)(2,1)S(1)} %gather.7, pred[32,2]{1,0:T(8,128)(4,1)S(1)} %copy.53, f32[32,2]{1,0:T(8,128)S(1)} %copy.50), kind=kLoop, calls=%fused_computation.16 | loop fusion | flops 458752 | bytes 524608 | tf_op jit(solution)/shard_map/reduce_sum | solution.py:77
  155.8 0.0 copy-done.1
  155.8 0.7 add_convert_fusion
  (8 shorter events, 0.1 us)
Async XLA Ops:
  6.5 4.7 %copy-start = (bf16[32,2048]{1,0:T(8,128)(2,1)S(1)}, bf16[32,2048]{1,0:T(8,128)(2,1)}, u32[]{:S(2)}) copy-start(bf16[32,2048]{1,0:T(8,128)(2,1)} %param.11) | copy-start | bytes 393220
  6.5 34.7 %all-gather.2.cloned.1.call-start = ((), (), s32[]{:S(2)}) async-start(), calls=%async_computation.2 | async-start | bytes 1572864 | tf_op jit(solution)/shard_map/all_gather | solution.py:62
  17.0 134.4 %all-reduce.3.cloned.1.call-start = ((), (), s32[]{:S(2)}) async-start(), calls=%async_computation.3 | async-start | bytes 2097152
  71.7 40.3 %copy-start.3 = (s32[32,2]{0,1:T(2,128)S(1)}, s32[32,2]{0,1:T(2,128)}, u32[]{:S(2)}) copy-start(s32[32,2]{0,1:T(2,128)} %param.19) | copy-start | bytes 772
  71.7 40.4 %copy-start.2 = (bf16[2048,16]{0,1:T(8,128)(2,1)S(1)}, bf16[2048,16]{0,1:T(8,128)(2,1)}, u32[]{:S(2)}) copy-start(bf16[2048,16]{0,1:T(8,128)(2,1)} %param.16) | copy-start | bytes 196612
  71.7 40.7 %copy-start.4 = (u32[32]{0:T(128)S(1)}, u32[32]{0:T(128)}, u32[]{:S(2)}) copy-start(u32[32]{0:T(128)} %constant.52) | copy-start | bytes 388
  71.7 84.1 %copy-start.1 = (bf16[32,2048]{1,0:T(8,128)(2,1)S(1)}, bf16[32,2048]{1,0:T(8,128)(2,1)}, u32[]{:S(2)}) copy-start(bf16[32,2048]{1,0:T(8,128)(2,1)} %param.10) | copy-start | bytes 393220
Sparse Core Ops, SparseCore 0:
  17.2 23.9 all-gather.1
  111.9 39.4 all-reduce.2
where the time goes:
time: 164 us; the launch traced here: 163 us
  waiting for transfers between devices  62.5 us (38%)
  blocking collectives  60.2 us (37%)
  between operations  14.2 us (9%)
  matrix products  11 us (7%)
  local copies, waits for them, and re-layouts  8.63 us (5%)
  other arithmetic  6.8 us (4%)
    unnamed x3, waiting for transfers between devices  38.4 us
    all_to_all x1, blocking collectives, on_device(): lax.all_to_all(stacked, 'expert', split_axis=0, concat_axis=0, tiled=True)  30.5 us
    all_to_all x1, blocking collectives, on_device(): lax.all_to_all(outbound, 'expert', split_axis=0, concat_axis=0, tiled=True)  29.7 us
    all_gather x1, waiting for transfers between devices, on_device(): stacked = lax.all_gather(outgoing[:, None], 'batch', axis=1, tiled=True)  24.1 us
    dot_general x1, matrix products, expert_term(): return jnp.dot(hidden, second_weight, preferred_element_type=jnp.float32)  10.3 us
  transfers between devices with their start and end apart: 2, of which 2 were waited for; matrix products, arithmetic and copies ran while one was open for 1% of the time, Pallas kernels for 0%

commit v1 on v0

--- a/solution.py
+++ b/solution.py
@@ -1,8 +1,11 @@
+import functools
 import math
 
 import jax
 import jax.numpy as jnp
 from jax import lax
+from jax.experimental import pallas as pl
+from jax.experimental.pallas import tpu as pltpu
 from jax.sharding import PartitionSpec as P
 
 D = 2048
@@ -47,7 +50,10 @@
     onehot = (flat_expert[:, None] == jnp.arange(experts_all, dtype=jnp.int32)[None, :]).astype(
         jnp.int32
     )
-    before = jnp.cumsum(onehot, axis=0) - onehot
+    earlier = jnp.tri(flat_expert.shape[0], k=-1, dtype=jnp.bfloat16)
+    before = jnp.dot(
+        earlier, onehot.astype(jnp.bfloat16), preferred_element_type=jnp.float32
+    ).astype(jnp.int32)
     slots = jnp.sum(before * onehot, axis=1)
     flat_owner = flat_expert * capacity + slots
     chosen = jnp.sum(
@@ -78,9 +84,377 @@
     return mixed.astype(jnp.bfloat16)
 
 
+GROUPS = 2
+STRIDE = 5
+TILE_ONE = 256
+TILE_TWO = 512
+PIECES = 4
+
+
+def fused_kernel(
+    experts,
+    cap,
+    resid_ref,
+    queries_ref,
+    keys_ref,
+    values_ref,
+    length_ref,
+    gain_ref,
+    router_ref,
+    ids_ref,
+    first_hbm,
+    second_hbm,
+    out_ref,
+    first,
+    second,
+    slots,
+    arrived,
+    block,
+    hidden,
+    mine,
+    sent,
+    taken,
+    back,
+    returned,
+    summed,
+    context,
+    first_sem,
+    second_sem,
+    out_send,
+    out_recv,
+    fwd_send,
+    fwd_recv,
+    sum_send,
+    sum_recv,
+    ret_send,
+    ret_recv,
+):
+    b = lax.axis_index("batch")
+    e = lax.axis_index("expert")
+    mesh_id = pl.DeviceIdType.MESH
+    rows = resid_ref.shape[0]
+    width = resid_ref.shape[1]
+    units = first.shape[1]
+    per = experts // GROUPS
+    piece = width // PIECES
+    unit_piece = units // PIECES
+    tiles_two = width // TILE_TWO
+    peer = 1 - b
+
+    def ahead(k):
+        return lax.rem(e + STRIDE * k, experts)
+
+    def behind(k):
+        return lax.rem(e + STRIDE * experts - STRIDE * k, experts)
+
+    barrier = pltpu.get_barrier_semaphore()
+
+    @pl.loop(1, experts)
+    def _(k):
+        pl.semaphore_signal(barrier, inc=1, device_id=(b, ahead(k)), device_id_type=mesh_id)
+
+    pl.semaphore_signal(barrier, inc=1, device_id=(peer, e), device_id_type=mesh_id)
+
+    def first_copy(p):
+        part = pl.ds(p * piece, piece)
+        return pltpu.make_async_copy(first_hbm.at[0, part, :], first.at[part, :], first_sem.at[p])
+
+    def second_copy(p):
+        part = pl.ds(p * unit_piece, unit_piece)
+        return pltpu.make_async_copy(
+            second_hbm.at[0, part, :], second.at[part, :], second_sem.at[p]
+        )
+
+    for p in range(PIECES):
+        first_copy(p).start()
+    for p in range(PIECES):
+        second_copy(p).start()
+
+    tokens = keys_ref.shape[1]
+    parts = []
+    for h in range(HEADS):
+        lanes = slice(h * HEAD_DIM, (h + 1) * HEAD_DIM)
+        parts.append(
+            lax.dot_general(
+                queries_ref[:, lanes],
+                keys_ref[0, :, lanes],
+                (((1,), (1,)), ((), ())),
+                preferred_element_type=jnp.float32,
+            )
+        )
+    scores = jnp.concatenate(parts, axis=0) / math.sqrt(HEAD_DIM)
+    visible = lax.broadcasted_iota(jnp.int32, scores.shape, 1) < length_ref[0]
+    scores = jnp.where(visible, scores, -1e30)
+    powers = jnp.exp(scores - jnp.max(scores, axis=-1, keepdims=True))
+    weights = (powers / jnp.sum(powers, axis=-1, keepdims=True)).astype(jnp.bfloat16)
+    for h in range(HEADS):
+        lanes = slice(h * HEAD_DIM, (h + 1) * HEAD_DIM)
+        context[:, lanes] = jnp.dot(
+            weights[h * rows : (h + 1) * rows, :],
+            values_ref[0, :, lanes],
+            preferred_element_type=jnp.float32,
+        )
+    total = resid_ref[...].astype(jnp.float32) + context[...]
+    summed[...] = total
+    center = jnp.mean(total, axis=-1, keepdims=True)
+    spread = jnp.mean((total - center) ** 2, axis=-1, keepdims=True)
+    normed = ((total - center) * lax.rsqrt(spread + 1e-05) * gain_ref[...]).astype(jnp.bfloat16)
+
+    count = experts * cap
+    column = lax.broadcasted_iota(jnp.int32, (rows, count), 1)
+    column_expert = lax.div(column, cap)
+    column_slot = lax.rem(column, cap).astype(jnp.float32)
+    named_0 = (ids_ref[:, 0:1] == column_expert).astype(jnp.float32)
+    named_1 = (ids_ref[:, 1:2] == column_expert).astype(jnp.float32)
+    earlier = (
+        lax.broadcasted_iota(jnp.int32, (rows, rows), 1)
+        < lax.broadcasted_iota(jnp.int32, (rows, rows), 0)
+    ).astype(jnp.bfloat16)
+    before = jnp.dot(
+        earlier, (named_0 + named_1).astype(jnp.bfloat16), preferred_element_type=jnp.float32
+    )
+    here = (before == column_slot).astype(jnp.float32)
+    place_0 = named_0 * here
+    place_1 = named_1 * here
+    filled = lax.dot_general(
+        (place_0 + place_1).astype(jnp.bfloat16),
+        normed,
+        (((0,), (0,)), ((), ())),
+        preferred_element_type=jnp.float32,
+    )
+    slots[...] = filled.reshape(experts, cap, width).astype(jnp.bfloat16)
+
+    def dispatch(k, target, at):
+        return pltpu.make_async_remote_copy(
+            src_ref=slots.at[target],
+            dst_ref=arrived.at[0, at],
+            send_sem=out_send.at[k],
+            recv_sem=out_recv.at[k],
+            device_id=(b, target),
+            device_id_type=mesh_id,
+        )
+
+    def forward(k):
+        return pltpu.make_async_remote_copy(
+            src_ref=arrived.at[0, k],
+            dst_ref=arrived.at[1, k],
+            send_sem=fwd_send.at[k],
+            recv_sem=fwd_recv.at[k],
+            device_id=(peer, e),
+            device_id_type=mesh_id,
+        )
+
+    def partial_copy(g, t):
+        part = (pl.ds(g * per, per), slice(None), pl.ds(t * TILE_TWO, TILE_TWO))
+        return pltpu.make_async_remote_copy(
+            src_ref=sent.at[part],
+            dst_ref=taken.at[part],
+            send_sem=sum_send.at[g, t],
+            recv_sem=sum_recv.at[g, t],
+            device_id=(peer, e),
+            device_id_type=mesh_id,
+        )
+
+    def give_back(k, target, at):
+        return pltpu.make_async_remote_copy(
+            src_ref=back.at[k],
+            dst_ref=returned.at[at],
+            send_sem=ret_send.at[k],
+            recv_sem=ret_recv.at[k],
+            device_id=(b, target),
+            device_id_type=mesh_id,
+        )
+
+    pl.semaphore_wait(barrier, experts)
+
+    @pl.loop(1, experts)
+    def _(k):
+        dispatch(k, ahead(k), k).start()
+
+    arrived[0, 0] = slots[e]
+    forward(0).start()
+
+    logits = jnp.dot(normed, router_ref[...], preferred_element_type=jnp.float32)
+    lane = lax.broadcasted_iota(jnp.int32, logits.shape, 1)
+    gate_0 = jax.nn.sigmoid(
+        jnp.sum(jnp.where(ids_ref[:, 0:1] == lane, logits, 0.0), axis=-1, keepdims=True)
+    )
+    gate_1 = jax.nn.sigmoid(
+        jnp.sum(jnp.where(ids_ref[:, 1:2] == lane, logits, 0.0), axis=-1, keepdims=True)
+    )
+
+    def pass_on(k):
+        dispatch(k, ahead(k), k).wait_recv()
+        forward(k).start()
+
+    def gather(g):
+        half = per * cap
+        for side in range(2):
+            block[side * half : (side + 1) * half, :] = (
+                arrived[side, g * per : (g + 1) * per]
+                .astype(jnp.float32)
+                .reshape(half, width)
+                .astype(jnp.bfloat16)
+            )
+
+    def into_hidden(g):
+        @pl.loop(0, units // TILE_ONE)
+        def _(t):
+            lanes = pl.ds(pl.multiple_of(t * TILE_ONE, TILE_ONE), TILE_ONE)
+            hidden[:, lanes] = jnp.maximum(
+                jnp.dot(block[...], first[:, lanes], preferred_element_type=jnp.float32), 0.0
+            ).astype(jnp.bfloat16)
+            if g + 1 < GROUPS:
+                pass_on((g + 1) * per + t)
+
+    def out_of_hidden(g):
+        half = per * cap
+        group = pl.ds(g * per, per)
+
+        @pl.loop(0, tiles_two)
+        def _(t):
+            lanes = pl.ds(pl.multiple_of(t * TILE_TWO, TILE_TWO), TILE_TWO)
+            result = jnp.dot(hidden[...], second[:, lanes], preferred_element_type=jnp.float32)
+            sent[group, :, lanes] = (
+                result[half:, :].reshape(per, cap, TILE_TWO).astype(jnp.bfloat16)
+            )
+            partial_copy(g, t).start()
+            mine[group, :, lanes] = (
+                result[:half, :].reshape(per, cap, TILE_TWO).astype(jnp.bfloat16)
+            )
+
+    def finish(g):
+        @pl.loop(0, tiles_two)
+        def _(t):
+            partial_copy(g, t).wait_recv()
+
+        def add(k):
+            return (mine[k].astype(jnp.float32) + taken[k].astype(jnp.float32)).astype(
+                jnp.bfloat16
+            )
+
+        if g == 0:
+            returned[e] = add(0)
+
+        @pl.loop(1 if g == 0 else g * per, (g + 1) * per)
+        def _(k):
+            back[k] = add(k)
+            give_back(k, behind(k), e).start()
+
+    @pl.loop(1, per)
+    def _(k):
+        pass_on(k)
+
+    for g in range(GROUPS):
+
+        @pl.loop(g * per, (g + 1) * per)
+        def _(k):
+            forward(k).wait_recv()
+
+        if g == 0:
+            for p in range(PIECES):
+                first_copy(p).wait()
+        gather(g)
+        into_hidden(g)
+        if g == 0:
+            for p in range(PIECES):
+                second_copy(p).wait()
+        if g > 0:
+            finish(g - 1)
+        out_of_hidden(g)
+    finish(GROUPS - 1)
+
+    @pl.loop(1, experts)
+    def _(k):
+        give_back(k, behind(k), ahead(k)).wait_recv()
+
+    answers = returned[...].astype(jnp.float32).reshape(count, width).astype(jnp.bfloat16)
+    chosen_0 = jnp.dot(
+        place_0.astype(jnp.bfloat16), answers, preferred_element_type=jnp.float32
+    )
+    chosen_1 = jnp.dot(
+        place_1.astype(jnp.bfloat16), answers, preferred_element_type=jnp.float32
+    )
+    out_ref[...] = (summed[...] + (gate_0 * chosen_0 + gate_1 * chosen_1)).astype(out_ref.dtype)
+
+    @pl.loop(1, experts)
+    def _(k):
+        dispatch(k, ahead(k), k).wait_send()
+        give_back(k, behind(k), e).wait_send()
+
+    @pl.loop(0, experts)
+    def _(k):
+        forward(k).wait_send()
+
+    for g in range(GROUPS):
+
+        @pl.loop(0, tiles_two)
+        def _(t):
+            partial_copy(g, t).wait_send()
+
+
+def fused(*arrays):
+    resid, router, w_in, w_out = arrays[0], arrays[6], arrays[7], arrays[8]
+    row_count, width = resid.shape
+    experts = router.shape[1]
+    cap = max(2, 4 * row_count // experts)
+    units = w_in.shape[2]
+    per = experts // GROUPS
+    tiles_two = width // TILE_TWO
+    bf16, f32 = jnp.bfloat16, jnp.float32
+    dma = pltpu.SemaphoreType.DMA
+    vmem = pl.BlockSpec(memory_space=pltpu.VMEM)
+    smem = pl.BlockSpec(memory_space=pltpu.SMEM)
+    hbm = pl.BlockSpec(memory_space=pl.ANY)
+    operands = (*arrays[:5], arrays[5].reshape(1, width), router, arrays[9], w_in, w_out)
+    return pl.pallas_call(
+        functools.partial(fused_kernel, experts, cap),
+        out_shape=jax.ShapeDtypeStruct((row_count, width), bf16),
+        in_specs=[vmem, vmem, vmem, vmem, smem, vmem, vmem, vmem, hbm, hbm],
+        out_specs=vmem,
+        scratch_shapes=[
+            pltpu.VMEM((width, units), bf16),
+            pltpu.VMEM((units, width), bf16),
+            pltpu.VMEM((experts, cap, width), bf16),
+            pltpu.VMEM((2, experts, cap, width), bf16),
+            pltpu.VMEM((2 * per * cap, width), bf16),
+            pltpu.VMEM((2 * per * cap, units), bf16),
+            pltpu.VMEM((experts, cap, width), bf16),
+            pltpu.VMEM((experts, cap, width), bf16),
+            pltpu.VMEM((experts, cap, width), bf16),
+            pltpu.VMEM((experts, cap, width), bf16),
+            pltpu.VMEM((experts, cap, width), bf16),
+            pltpu.VMEM((row_count, width), f32),
+            pltpu.VMEM((row_count, width), f32),
+            dma((PIECES,)),
+            dma((PIECES,)),
+            dma((experts,)),
+            dma((experts,)),
+            dma((experts,)),
+            dma((experts,)),
+            dma((GROUPS, tiles_two)),
+            dma((GROUPS, tiles_two)),
+            dma((experts,)),
+            dma((experts,)),
+        ],
+        compiler_params=pltpu.CompilerParams(
+            collective_id=0, has_side_effects=True, vmem_limit_bytes=50 * 2**20
+        ),
+    )(*operands)
+
+
+def per_device(mesh, *arrays):
+    row_count = arrays[0].shape[0]
+    experts = mesh.shape["expert"]
+    cap = max(2, 4 * row_count // arrays[6].shape[1])
+    if mesh.shape["batch"] == 2 and arrays[6].shape[1] == experts and cap == 8 and experts == 16:
+        return fused(*arrays)
+    return on_device(*arrays)
+
+
 def solution(mesh):
     return jax.shard_map(
-        on_device,
+        functools.partial(per_device, mesh),
         mesh=mesh,
         in_specs=(
             P(("batch", "expert"), None),

time: 164 us -> 54.9 us (0.33)
  the two profiles are of different devices: /device:TPU:0 before, /device:TPU:5 now
where the time goes in v1:
time: 54.9 us; the launch traced here: 54.6 us
  Pallas kernels  47.1 us (86%)
  local copies, waits for them, and re-layouts  6.84 us (12%)
  between operations  0.68 us (1%)
    pallas_call x1, Pallas kernels, fused(): pl.pallas_call(functools.partial(fused_kernel, experts, cap), out_shape=j...  47.1 us
    unnamed x13, local copies, waits for them, and re-layouts  6.84 us

profile of v1, /device:TPU:5, one launch (start us, length us, event | category | flops | bytes accessed | tf_op | source)
XLA Modules:
  0.0 54.6 jit_solution(15932118171519547672)
XLA Ops:
  0.7 0.8 %copy.12.ids_ref = s32[32,2]{1,0:T(8,128)S(1)} copy(s32[32,2]{0,1:T(2,128)} %param.19) | data formatting | bytes 512 | tf_op args[9]
  1.4 1.1 %copy.11.router_ref = bf16[2048,16]{1,0:T(8,128)(2,1)S(1)} copy(bf16[2048,16]{0,1:T(8,128)(2,1)} %param.16) | data formatting | bytes 131072 | tf_op args[6]
  2.5 0.0 copy-start
  2.5 0.9 %copy-done = bf16[32,2048]{1,0:T(8,128)(2,1)S(1)} copy-done((bf16[32,2048]{1,0:T(8,128)(2,1)S(1)}, bf16[32,2048]{1,0:T(8,128)(2,1)}, u32[]{:S(2)}) %copy-start) | copy-done | bytes 131096
  3.4 0.0 copy-start.1
  3.4 0.9 %copy-done.1 = bf16[32,2048]{1,0:T(8,128)(2,1)S(1)} copy-done((bf16[32,2048]{1,0:T(8,128)(2,1)S(1)}, bf16[32,2048]{1,0:T(8,128)(2,1)}, u32[]{:S(2)}) %copy-start.1) | copy-done | bytes 131096
  4.3 0.0 copy-start.2
  4.3 0.9 %copy-done.2 = bf16[1,32,2048]{2,1,0:T(8,128)(2,1)S(1)} copy-done((bf16[1,32,2048]{2,1,0:T(8,128)(2,1)S(1)}, bf16[1,32,2048]{2,1,0:T(8,128)(2,1)}, u32[]{:S(2)}) %copy-start.2) | copy-done | bytes 131096
  5.2 0.0 copy-start.3
  5.3 0.9 %copy-done.3 = bf16[1,32,2048]{2,1,0:T(8,128)(2,1)S(1)} copy-done((bf16[1,32,2048]{2,1,0:T(8,128)(2,1)S(1)}, bf16[1,32,2048]{2,1,0:T(8,128)(2,1)}, u32[]{:S(2)}) %copy-start.3) | copy-done | bytes 131096
  6.2 0.0 copy-start.4
  6.2 0.7 %copy-done.4 = f32[2048]{0:T(1024)S(1)} copy-done((f32[2048]{0:T(1024)S(1)}, f32[2048]{0:T(1024)}, u32[]{:S(2)}) %copy-start.4) | copy-done | bytes 8216
  6.9 47.1 %shard_map.100 = bf16[32,2048]{1,0:T(8,128)(2,1)S(1)} custom-call(bf16[32,2048]{1,0:T(8,128)(2,1)S(1)} %copy-done, bf16[32,2048]{1,0:T(8,128)(2,1)S(1)} %copy-done.1, bf16[1,32,2048]{2,1,0:T(8,128)(2,1)S(1)} %copy-done.2, bf16[1,32,2048]{2,1,0:T(8,128)(2,1)S(1)} %copy-done.3, s32[1]{0:T(128)S(6)} %copy.14.length_ref, f32[1,2048]{1,0:T(1,128)S(1)} %bitcast.1, ...), custom_call_target="tpu_custom_call" | custom-call | tf_op jit(solution)/shard_map/pallas_call | solution.py:410
  53.9 0.7 %copy.15 = bf16[32,2048]{1,0:T(8,128)(2,1)} copy(bf16[32,2048]{1,0:T(8,128)(2,1)S(1)} %shard_map.100) | data formatting | bytes 262144
Async XLA Ops:
  2.5 0.9 %copy-start = (bf16[32,2048]{1,0:T(8,128)(2,1)S(1)}, bf16[32,2048]{1,0:T(8,128)(2,1)}, u32[]{:S(2)}) copy-start(bf16[32,2048]{1,0:T(8,128)(2,1)} %resid_ref.1) | copy-start | bytes 393220
  3.4 0.9 %copy-start.1 = (bf16[32,2048]{1,0:T(8,128)(2,1)S(1)}, bf16[32,2048]{1,0:T(8,128)(2,1)}, u32[]{:S(2)}) copy-start(bf16[32,2048]{1,0:T(8,128)(2,1)} %queries_ref.1) | copy-start | bytes 393220
  4.3 0.9 %copy-start.2 = (bf16[1,32,2048]{2,1,0:T(8,128)(2,1)S(1)}, bf16[1,32,2048]{2,1,0:T(8,128)(2,1)}, u32[]{:S(2)}) copy-start(bf16[1,32,2048]{2,1,0:T(8,128)(2,1)} %keys_ref.1) | copy-start | bytes 393220
  5.2 0.9 %copy-start.3 = (bf16[1,32,2048]{2,1,0:T(8,128)(2,1)S(1)}, bf16[1,32,2048]{2,1,0:T(8,128)(2,1)}, u32[]{:S(2)}) copy-start(bf16[1,32,2048]{2,1,0:T(8,128)(2,1)} %values_ref.1) | copy-start | bytes 393220
  6.2 0.7 %copy-start.4 = (f32[2048]{0:T(1024)S(1)}, f32[2048]{0:T(1024)}, u32[]{:S(2)}) copy-start(f32[2048]{0:T(1024)} %param.15) | copy-start | bytes 24580

commit v2 on v1

--- a/solution.py
+++ b/solution.py
@@ -84,9 +84,11 @@
     return mixed.astype(jnp.bfloat16)
 
 
-GROUPS = 2
-STRIDE = 5
-TILE_ONE = 256
+PLANES = 4
+ORDER = (0, 2, 1, 3)
+GROUPS = len(ORDER)
+LAG = 2
+TILE_ONE = 512
 TILE_TWO = 512
 PIECES = 4
 
@@ -94,14 +96,14 @@
 def fused_kernel(
     experts,
     cap,
-    resid_ref,
-    queries_ref,
-    keys_ref,
-    values_ref,
     length_ref,
-    gain_ref,
-    router_ref,
-    ids_ref,
+    resid_hbm,
+    queries_hbm,
+    keys_hbm,
+    values_hbm,
+    gain_hbm,
+    router_hbm,
+    ids_hbm,
     first_hbm,
     second_hbm,
     out_ref,
@@ -118,6 +120,14 @@
     returned,
     summed,
     context,
+    resid_ref,
+    queries_ref,
+    keys_ref,
+    values_ref,
+    gain_ref,
+    router_ref,
+    ids_ref,
+    input_sem,
     first_sem,
     second_sem,
     out_send,
@@ -141,19 +151,43 @@
     tiles_two = width // TILE_TWO
     peer = 1 - b
 
-    def ahead(k):
-        return lax.rem(e + STRIDE * k, experts)
-
-    def behind(k):
-        return lax.rem(e + STRIDE * experts - STRIDE * k, experts)
+    plane = lax.div(e, per)
+    spot = lax.rem(e, per)
+
+    def ahead(g, j):
+        return lax.rem(plane + ORDER[g], PLANES) * per + lax.rem(spot + j, per)
+
+    def behind(g, j):
+        return lax.rem(plane + PLANES - ORDER[g], PLANES) * per + lax.rem(spot + per - j, per)
 
     barrier = pltpu.get_barrier_semaphore()
 
-    @pl.loop(1, experts)
-    def _(k):
-        pl.semaphore_signal(barrier, inc=1, device_id=(b, ahead(k)), device_id_type=mesh_id)
+    for g in range(GROUPS):
+
+        @pl.loop(1 if g == 0 else 0, per)
+        def _(j):
+            pl.semaphore_signal(
+                barrier, inc=1, device_id=(b, ahead(g, j)), device_id_type=mesh_id
+            )
 
     pl.semaphore_signal(barrier, inc=1, device_id=(peer, e), device_id_type=mesh_id)
+
+    inputs = [
+        pltpu.make_async_copy(source, target, input_sem.at[i])
+        for i, (source, target) in enumerate(
+            (
+                (queries_hbm, queries_ref),
+                (keys_hbm, keys_ref),
+                (values_hbm, values_ref),
+                (resid_hbm, resid_ref),
+                (gain_hbm, gain_ref),
+                (ids_hbm, ids_ref),
+                (router_hbm, router_ref),
+            )
+        )
+    ]
+    for copy in inputs:
+        copy.start()
 
     def first_copy(p):
         part = pl.ds(p * piece, piece)
@@ -170,7 +204,9 @@
     for p in range(PIECES):
         second_copy(p).start()
 
-    tokens = keys_ref.shape[1]
+    for copy in inputs:
+        copy.wait()
+
     parts = []
     for h in range(HEADS):
         lanes = slice(h * HEAD_DIM, (h + 1) * HEAD_DIM)
@@ -201,36 +237,38 @@
     normed = ((total - center) * lax.rsqrt(spread + 1e-05) * gain_ref[...]).astype(jnp.bfloat16)
 
     count = experts * cap
-    column = lax.broadcasted_iota(jnp.int32, (rows, count), 1)
-    column_expert = lax.div(column, cap)
-    column_slot = lax.rem(column, cap).astype(jnp.float32)
-    named_0 = (ids_ref[:, 0:1] == column_expert).astype(jnp.float32)
-    named_1 = (ids_ref[:, 1:2] == column_expert).astype(jnp.float32)
-    earlier = (
-        lax.broadcasted_iota(jnp.int32, (rows, rows), 1)
-        < lax.broadcasted_iota(jnp.int32, (rows, rows), 0)
-    ).astype(jnp.bfloat16)
-    before = jnp.dot(
-        earlier, (named_0 + named_1).astype(jnp.bfloat16), preferred_element_type=jnp.float32
-    )
-    here = (before == column_slot).astype(jnp.float32)
+    bf16 = jnp.bfloat16
+
+    def product(left, right, left_axis, right_axis):
+        return lax.dot_general(
+            left.astype(bf16),
+            right.astype(bf16),
+            (((left_axis,), (right_axis,)), ((), ())),
+            preferred_element_type=jnp.float32,
+        )
+
+    line = lax.broadcasted_iota(jnp.int32, (count, rows), 0)
+    line_expert = lax.div(line, cap)
+    line_slot = lax.rem(line, cap).astype(jnp.float32)
+    named_0 = (ids_ref[0:1, :] == line_expert).astype(jnp.float32)
+    named_1 = (ids_ref[1:2, :] == line_expert).astype(jnp.float32)
+    row_from = lax.broadcasted_iota(jnp.int32, (rows, rows), 0)
+    row_to = lax.broadcasted_iota(jnp.int32, (rows, rows), 1)
+    before = product(named_0 + named_1, (row_from < row_to).astype(jnp.float32), 1, 0)
+    here = (before == line_slot).astype(jnp.float32)
     place_0 = named_0 * here
     place_1 = named_1 * here
-    filled = lax.dot_general(
-        (place_0 + place_1).astype(jnp.bfloat16),
-        normed,
-        (((0,), (0,)), ((), ())),
-        preferred_element_type=jnp.float32,
-    )
+    filled = product(place_0 + place_1, normed, 1, 0)
     slots[...] = filled.reshape(experts, cap, width).astype(jnp.bfloat16)
 
-    def dispatch(k, target, at):
+    def dispatch(g, j):
+        k = g * per + j
         return pltpu.make_async_remote_copy(
-            src_ref=slots.at[target],
-            dst_ref=arrived.at[0, at],
+            src_ref=slots.at[ahead(g, j)],
+            dst_ref=arrived.at[0, k],
             send_sem=out_send.at[k],
             recv_sem=out_recv.at[k],
-            device_id=(b, target),
+            device_id=(b, ahead(g, j)),
             device_id_type=mesh_id,
         )
 
@@ -255,37 +293,45 @@
             device_id_type=mesh_id,
         )
 
-    def give_back(k, target, at):
+    def give_back(g, j, at):
+        k = g * per + j
         return pltpu.make_async_remote_copy(
             src_ref=back.at[k],
             dst_ref=returned.at[at],
             send_sem=ret_send.at[k],
             recv_sem=ret_recv.at[k],
-            device_id=(b, target),
+            device_id=(b, behind(g, j)),
             device_id_type=mesh_id,
         )
 
     pl.semaphore_wait(barrier, experts)
 
-    @pl.loop(1, experts)
-    def _(k):
-        dispatch(k, ahead(k), k).start()
+    for g in range(2):
+
+        @pl.loop(1 if g == 0 else 0, per)
+        def _(j):
+            dispatch(g, j).start()
 
     arrived[0, 0] = slots[e]
     forward(0).start()
 
-    logits = jnp.dot(normed, router_ref[...], preferred_element_type=jnp.float32)
-    lane = lax.broadcasted_iota(jnp.int32, logits.shape, 1)
-    gate_0 = jax.nn.sigmoid(
-        jnp.sum(jnp.where(ids_ref[:, 0:1] == lane, logits, 0.0), axis=-1, keepdims=True)
-    )
-    gate_1 = jax.nn.sigmoid(
-        jnp.sum(jnp.where(ids_ref[:, 1:2] == lane, logits, 0.0), axis=-1, keepdims=True)
-    )
-
-    def pass_on(k):
-        dispatch(k, ahead(k), k).wait_recv()
-        forward(k).start()
+    logits = product(normed, router_ref[...], 1, 1)
+    number = lax.broadcasted_iota(jnp.int32, (experts, rows), 0)
+    unit = (row_from == row_to).astype(jnp.float32)
+
+    def gate(at):
+        named = (ids_ref[at : at + 1, :] == number).astype(jnp.float32)
+        turned = product(unit, named, 1, 1)
+        return jax.nn.sigmoid(jnp.sum(turned * logits, axis=-1, keepdims=True))
+
+    gate_0 = gate(0)
+    gate_1 = gate(1)
+
+    def pass_on(g, j):
+        dispatch(g, j).wait_recv()
+        forward(g * per + j).start()
+        if 1 <= g < GROUPS - 1:
+            dispatch(g + 1, j).start()
 
     def gather(g):
         half = per * cap
@@ -304,8 +350,8 @@
             hidden[:, lanes] = jnp.maximum(
                 jnp.dot(block[...], first[:, lanes], preferred_element_type=jnp.float32), 0.0
             ).astype(jnp.bfloat16)
-            if g + 1 < GROUPS:
-                pass_on((g + 1) * per + t)
+            if g + 2 < GROUPS:
+                pass_on(g + 2, t)
 
     def out_of_hidden(g):
         half = per * cap
@@ -322,28 +368,43 @@
             mine[group, :, lanes] = (
                 result[:half, :].reshape(per, cap, TILE_TWO).astype(jnp.bfloat16)
             )
-
-    def finish(g):
+            if g >= LAG:
+
+                @pl.when(t == 0)
+                def _():
+                    await_partials(g - LAG)
+
+                finish(g - LAG, t)
+
+    def await_partials(g):
         @pl.loop(0, tiles_two)
         def _(t):
             partial_copy(g, t).wait_recv()
 
-        def add(k):
-            return (mine[k].astype(jnp.float32) + taken[k].astype(jnp.float32)).astype(
-                jnp.bfloat16
-            )
-
-        if g == 0:
-            returned[e] = add(0)
-
-        @pl.loop(1 if g == 0 else g * per, (g + 1) * per)
-        def _(k):
-            back[k] = add(k)
-            give_back(k, behind(k), e).start()
+    def finish(g, j):
+        k = g * per + j
+        both = (mine[k].astype(jnp.float32) + taken[k].astype(jnp.float32)).astype(jnp.bfloat16)
+        if g > 0:
+            back[k] = both
+            give_back(g, j, e).start()
+        else:
+
+            @pl.when(j == 0)
+            def _():
+                returned[e] = both
+
+            @pl.when(j > 0)
+            def _():
+                back[k] = both
+                give_back(g, j, e).start()
 
     @pl.loop(1, per)
-    def _(k):
-        pass_on(k)
+    def _(j):
+        pass_on(0, j)
+
+    @pl.loop(0, per)
+    def _(j):
+        pass_on(1, j)
 
     for g in range(GROUPS):
 
@@ -359,28 +420,31 @@
         if g == 0:
             for p in range(PIECES):
                 second_copy(p).wait()
-        if g > 0:
-            finish(g - 1)
         out_of_hidden(g)
-    finish(GROUPS - 1)
-
-    @pl.loop(1, experts)
-    def _(k):
-        give_back(k, behind(k), ahead(k)).wait_recv()
+    for g in range(GROUPS - LAG, GROUPS):
+        await_partials(g)
+
+        @pl.loop(0, per)
+        def _(j):
+            finish(g, j)
+
+    for g in range(GROUPS):
+
+        @pl.loop(1 if g == 0 else 0, per)
+        def _(j):
+            give_back(g, j, ahead(g, j)).wait_recv()
 
     answers = returned[...].astype(jnp.float32).reshape(count, width).astype(jnp.bfloat16)
-    chosen_0 = jnp.dot(
-        place_0.astype(jnp.bfloat16), answers, preferred_element_type=jnp.float32
-    )
-    chosen_1 = jnp.dot(
-        place_1.astype(jnp.bfloat16), answers, preferred_element_type=jnp.float32
-    )
+    chosen_0 = product(place_0, answers, 0, 0)
+    chosen_1 = product(place_1, answers, 0, 0)
     out_ref[...] = (summed[...] + (gate_0 * chosen_0 + gate_1 * chosen_1)).astype(out_ref.dtype)
 
-    @pl.loop(1, experts)
-    def _(k):
-        dispatch(k, ahead(k), k).wait_send()
-        give_back(k, behind(k), e).wait_send()
+    for g in range(GROUPS):
+
+        @pl.loop(1 if g == 0 else 0, per)
+        def _(j):
+            dispatch(g, j).wait_send()
+            give_back(g, j, e).wait_send()
 
     @pl.loop(0, experts)
     def _(k):
@@ -405,12 +469,13 @@
     dma = pltpu.SemaphoreType.DMA
     vmem = pl.BlockSpec(memory_space=pltpu.VMEM)
     smem = pl.BlockSpec(memory_space=pltpu.SMEM)
-    hbm = pl.BlockSpec(memory_space=pl.ANY)
-    operands = (*arrays[:5], arrays[5].reshape(1, width), router, arrays[9], w_in, w_out)
+    hbm = pl.BlockSpec(memory_space=pltpu.HBM)
+    small = (*arrays[:4], arrays[5].reshape(1, width), router.T, arrays[9].T)
+    operands = (arrays[4], *small, w_in, w_out)
     return pl.pallas_call(
         functools.partial(fused_kernel, experts, cap),
         out_shape=jax.ShapeDtypeStruct((row_count, width), bf16),
-        in_specs=[vmem, vmem, vmem, vmem, smem, vmem, vmem, vmem, hbm, hbm],
+        in_specs=[smem] + [hbm] * 9,
         out_specs=vmem,
         scratch_shapes=[
             pltpu.VMEM((width, units), bf16),
@@ -426,6 +491,8 @@
             pltpu.VMEM((experts, cap, width), bf16),
             pltpu.VMEM((row_count, width), f32),
             pltpu.VMEM((row_count, width), f32),
+            *(pltpu.VMEM(array.shape, array.dtype) for array in small),
+            dma((len(small),)),
             dma((PIECES,)),
             dma((PIECES,)),
             dma((experts,)),
@@ -438,7 +505,7 @@
             dma((experts,)),
         ],
         compiler_params=pltpu.CompilerParams(
-            collective_id=0, has_side_effects=True, vmem_limit_bytes=50 * 2**20
+            collective_id=0, has_side_effects=True, vmem_limit_bytes=62 * 2**20
         ),
     )(*operands)
 

time: 54.9 us -> 51 us (0.929)
  the two profiles are of different devices: /device:TPU:5 before, /device:TPU:0 now
where the time goes in v2:
time: 51 us; the launch traced here: 50.8 us
  Pallas kernels  48.6 us (95%)
  local copies, waits for them, and re-layouts  1.57 us (3%)
  between operations  0.66 us (1%)
    pallas_call x1, Pallas kernels, fused(): pl.pallas_call(functools.partial(fused_kernel, experts, cap), out_shape=j...  48.6 us
    unnamed x1, local copies, waits for them, and re-layouts  1.57 us

profile of v2, /device:TPU:0, one launch (start us, length us, event | category | flops | bytes accessed | tf_op | source)
XLA Modules:
  0.0 50.8 jit_solution(8656667064060452459)
XLA Ops:
  0.7 48.6 %shard_map.100 = bf16[32,2048]{1,0:T(8,128)(2,1)} custom-call(s32[1]{0:T(128)S(6)} %copy.12.length_ref, bf16[32,2048]{1,0:T(8,128)(2,1)} %resid_hbm.1, bf16[32,2048]{1,0:T(8,128)(2,1)} %queries_hbm.1, bf16[1,32,2048]{2,1,0:T(8,128)(2,1)} %keys_hbm.1, bf16[1,32,2048]{2,1,0:T(8,128)(2,1)} %values_hbm.1, f32[1,2048]{1,0:T(1,128)} %bitcast.4, ...), custom_call_target="tpu_custom_call" | custom-call | tf_op jit(solution)/shard_map/pallas_call | solution.py:475
  49.3 1.6 %copy.13 = bf16[32,2048]{1,0:T(8,128)(2,1)} copy(bf16[32,2048]{1,0:T(8,128)(2,1)} %shard_map.100) | data formatting | bytes 262144
